TPU v7x, 32 devices: a whole 2x2x4 slice. The times are simulated.
32 devices in a mesh: groups: 2 (over y), replica: 8 (over z, x), tensor: 2 (over core).
Axes of the slice: x: 2, y: 2, z: 4, core: 2. Of those that a mesh axis runs over, the one named last changes fastest.
Arguments:
- hidden: bfloat16 [192, 8192], P(('groups', 'replica'), 'tensor'), parts along dimension 0, may hold values from -6 to 6
- rollout_lengths: int32 [64], P('groups'), parts along dimension 0, may hold values from 1 to 3
- source_replica: int32 [64], P('groups'), parts along dimension 0, may hold values from 0 to 7, as said below
- page_table: int32 [64, 3], P('groups'), parts along dimension 0, may hold values from 0 to 191, as said below
- x_new: bfloat16 [2, 64, 8192], P(None, 'groups', 'tensor'), parts along dimension 1, may hold values from -6 to 6
- norm_attn: float32 [8192], P('tensor'), may hold values from 0.5 to 1.5
- norm_ffn: float32 [8192], P('tensor'), may hold values from 0.5 to 1.5
- w_query: bfloat16 [8192, 8192], P('tensor', 'replica'), may hold values from -0.0625 to 0.0625
- w_keyval: bfloat16 [8192, 2, 8192], P('tensor', None, 'replica'), may hold values from -0.0625 to 0.0625
- qkv_bias: float32 [3, 8192], P(None, 'replica'), may hold values from -7 to 7
- w_out: bfloat16 [8192, 8192], P('replica', 'tensor'), may hold values from -0.0625 to 0.0625
- w_gateup: bfloat16 [8192, 2, 12288], P('tensor', None, 'replica'), may hold values from -0.0625 to 0.0625
- w_down: bfloat16 [12288, 8192], P('replica', 'tensor'), may hold values from -0.0546875 to 0.0546875
Outputs:
- decoded: bfloat16 [2, 64, 8192], P(None, 'groups', 'tensor'), parts along dimension 1
- kv_pool: bfloat16 [2, 384, 8192], P(None, ('groups', 'tensor'), 'replica'), parts along dimension 1
There are 2 independent parts, one for each index of `groups`. A program takes and returns all parts, laid end to end along the dimension named above; an argument that names none is the same for every part. Nothing has to cross between parts.
Inputs may be any that keep to these rules, and one draw needn't show every extreme that they name: `source_replica`: rollouts on one source replica have together at most 12 cached rows, and in every draw some source replica holds exactly 12; at most 4 rollouts share a source. `page_table`: all entries are distinct.
All inputs are finite; a program needn't handle non-finite values.
Results may differ from a plain program's by a relative error of at most 0.0169.
Values may be sent and summed in bfloat16 or wider, within the bound.
A program may use at most 256 MiB of HBM per device.

v0:
```python
import jax
import jax.numpy as jnp
from jax import lax
from jax.sharding import PartitionSpec as P

D = 8192
HD = 128
STEPS = 2


EPSILON = 1e-06
NEGATIVE = -1e30


def partner(array, axis, bit):
    return lax.ppermute(array, axis, [(i, i ^ 1 << bit) for i in range(lax.axis_size(axis))])


def merged(part, axis, combine):
    gathered = jax.tree.map(lambda a: lax.all_gather(a, axis), part)

    def take(source):
        return jax.tree.map(lambda a: lax.dynamic_index_in_dim(a, source, 0, False), gathered)

    return lax.fori_loop(
        1, lax.axis_size(axis), lambda source, state: combine(state, take(source)), take(0)
    )


def per_device(
    hidden,
    rollout_lengths,
    source_replica,
    page_table,
    x_new,
    norm_attn,
    norm_ffn,
    w_query,
    w_keyval,
    qkv_bias,
    w_out,
    w_gateup,
    w_down,
):
    replicas = lax.axis_size("replica")
    slots = hidden.shape[0]
    half_width = hidden.shape[1]
    columns = w_query.shape[1]
    rollouts = rollout_lengths.shape[0]
    longest = page_table.shape[1]
    pool_rows = 2 * rollouts * longest
    half_rows = pool_rows // 2
    units = w_down.shape[0]
    keyval_flat = w_keyval.reshape(half_width, 2 * columns)
    sequence = jnp.arange(rollouts, dtype=jnp.int32)
    earlier = (source_replica[:, None] == source_replica[None, :]) & (
        sequence[None, :] < sequence[:, None]
    )
    offsets = jnp.sum(jnp.where(earlier, rollout_lengths[None, :], 0), axis=1)
    places = jnp.arange(longest, dtype=jnp.int32)
    is_valid = places[None, :] < rollout_lengths[:, None]
    targets = jnp.where(is_valid, page_table, pool_rows)
    owners = (
        jnp.full((pool_rows,), -1, jnp.int32)
        .at[targets.reshape(-1)]
        .set(jnp.broadcast_to(sequence[:, None], (rollouts, longest)).reshape(-1), mode="drop")
    )
    empty = (jnp.zeros((pool_rows, 2 * columns), jnp.float32), jnp.zeros((pool_rows,), jnp.float32))
    slot_index = source_replica[:, None] * slots + offsets[:, None] + places[None, :]
    slot_index = jnp.where(is_valid, slot_index, replicas * slots)
    lookup = (
        jnp.full((replicas * slots,), pool_rows, jnp.int32)
        .at[slot_index.reshape(-1)]
        .set(targets.reshape(-1), mode="drop")
    )
    block_rows = lax.all_gather(hidden, "replica", axis=0, tiled=True)
    wide = block_rows.astype(jnp.float32)
    make_scaled = (wide * norm_attn).astype(jnp.bfloat16)
    partial_kv = jnp.dot(make_scaled, keyval_flat, preferred_element_type=jnp.float32)
    make_squares = jnp.sum(wide * wide, axis=1)
    part_pool = empty[0].at[lookup].add(partial_kv, mode="drop")
    stat_pool = empty[1].at[lookup].add(make_squares, mode="drop")
    part_half, stat_half = (
        lax.psum_scatter(
            part_pool.astype(jnp.bfloat16), "tensor", scatter_dimension=0, tiled=True
        ).astype(jnp.float32),
        lax.psum_scatter(
            stat_pool.astype(jnp.bfloat16), "tensor", scatter_dimension=0, tiled=True
        ).astype(jnp.float32),
    )
    tensor_index = lax.axis_index("tensor")
    owner_half = lax.dynamic_slice_in_dim(owners, tensor_index * half_rows, half_rows)
    filled = (owner_half >= 0)[:, None]
    row_scale = lax.rsqrt(stat_half / D + EPSILON)[:, None]
    kv_half = jnp.where(
        filled, row_scale * part_half + qkv_bias[1:].reshape(1, 2 * columns), 0.0
    ).astype(jnp.bfloat16)
    kv_out = jnp.transpose(kv_half.reshape(half_rows, 2, columns), (1, 0, 2))
    cache_keys = kv_half[:, :columns].astype(jnp.float32)
    cache_vals = kv_half[:, columns:].astype(jnp.float32)
    heads_here = max(1, columns // HD)
    piece_width = columns // heads_here
    group_size = HD // piece_width
    bit_count = group_size.bit_length() - 1
    inverse = 1.0 / jnp.sqrt(jnp.float32(HD))
    onehot = owner_half[:, None] == sequence[None, :]
    onehot_half = onehot.astype(jnp.bfloat16)
    onehot_wide = onehot.astype(jnp.float32)
    keep_new = tensor_index == 0

    def spread_out(values):
        return jnp.repeat(values, piece_width, axis=-1)

    def combine(first, second):
        peak_val = jnp.maximum(first[0], second[0])
        scale_one = jnp.exp(first[0] - peak_val)
        scale_two = jnp.exp(second[0] - peak_val)
        return (
            peak_val,
            first[1] * scale_one + second[1] * scale_two,
            first[2] * spread_out(scale_one) + second[2] * spread_out(scale_two),
        )

    new_keys = []
    new_vals = []
    decoded_rows = []
    for turn_index in range(STEPS):
        x_wide = x_new[turn_index].astype(jnp.float32)
        scaled = (x_wide * norm_attn).astype(jnp.bfloat16)
        query_part = jnp.dot(scaled, w_query, preferred_element_type=jnp.float32)
        keyval_part = jnp.dot(scaled, keyval_flat, preferred_element_type=jnp.float32)
        squares = jnp.sum(x_wide * x_wide, axis=1)
        query_part, keyval_part, squares = lax.psum((query_part, keyval_part, squares), "tensor")
        step_scale = lax.rsqrt(squares / D + EPSILON)[:, None]
        query = (step_scale * query_part + qkv_bias[0]).astype(jnp.bfloat16)
        new_keys.append((step_scale * keyval_part[:, :columns] + qkv_bias[1]).astype(jnp.bfloat16))
        new_vals.append((step_scale * keyval_part[:, columns:] + qkv_bias[2]).astype(jnp.bfloat16))
        query_wide = query.astype(jnp.float32)
        picked_query = jnp.dot(onehot_half, query, preferred_element_type=jnp.float32)
        cache_scores = jnp.sum(
            (picked_query * cache_keys).reshape(half_rows, heads_here, piece_width), axis=-1
        )
        new_scores = jnp.stack(
            [
                jnp.sum(
                    (query_wide * key_row.astype(jnp.float32)).reshape(
                        rollouts, heads_here, piece_width
                    ),
                    axis=-1,
                )
                for key_row in new_keys
            ]
        )
        for bit_index in range(bit_count):
            swapped = partner((cache_scores, new_scores), "replica", bit_index)
            cache_scores = cache_scores + swapped[0]
            new_scores = new_scores + swapped[1]
        cache_scores = jnp.where(filled, cache_scores * inverse, NEGATIVE)
        new_scores = jnp.where(keep_new, new_scores * inverse, NEGATIVE)
        segment_top = jnp.max(
            jnp.where(onehot[:, :, None], cache_scores[:, None, :], NEGATIVE), axis=0
        )
        peak_val = jnp.maximum(segment_top, jnp.max(new_scores, axis=0))
        row_peak = jnp.dot(onehot_wide, peak_val, precision=lax.Precision.HIGHEST)
        cache_weights = jnp.exp(cache_scores - row_peak)
        new_weights = jnp.where(keep_new, jnp.exp(new_scores - peak_val[None]), 0.0)
        totals = jnp.dot(onehot_wide.T, cache_weights, precision=lax.Precision.HIGHEST) + jnp.sum(
            new_weights, axis=0
        )
        cache_rounded = spread_out(cache_weights.astype(jnp.bfloat16).astype(jnp.float32))
        accum = jnp.dot(onehot_wide.T, cache_rounded * cache_vals, precision=lax.Precision.HIGHEST)
        for item_index in range(len(new_vals)):
            new_rounded = spread_out(
                new_weights[item_index].astype(jnp.bfloat16).astype(jnp.float32)
            )
            accum = accum + new_rounded * new_vals[item_index].astype(jnp.float32)
        peak_all, total_all, accum_all = merged((peak_val, totals, accum), "tensor", combine)
        attended = (accum_all / spread_out(total_all)).astype(jnp.bfloat16)
        attn_part = jnp.dot(attended, w_out, preferred_element_type=jnp.float32)
        middle = x_wide + lax.psum(attn_part, "replica")
        scaled_mid = (middle * norm_ffn).astype(jnp.bfloat16)
        gate_up = jnp.dot(
            scaled_mid, w_gateup.reshape(half_width, 2 * units), preferred_element_type=jnp.float32
        )
        mid_squares = jnp.sum(middle * middle, axis=1)
        gate_up, mid_squares = lax.psum((gate_up, mid_squares), "tensor")
        mid_scale = lax.rsqrt(mid_squares / D + EPSILON)[:, None]
        gate_vals = mid_scale * gate_up[:, :units]
        up_vals = mid_scale * gate_up[:, units:]
        hidden_mid = (jax.nn.silu(gate_vals) * up_vals).astype(jnp.bfloat16)
        down_part = jnp.dot(hidden_mid, w_down, preferred_element_type=jnp.float32)
        result = middle + lax.psum(down_part, "replica")
        decoded_rows.append(result.astype(jnp.bfloat16))
    return (jnp.stack(decoded_rows), kv_out)


def solution(mesh):
    placed = (
        P(("groups", "replica"), "tensor"),
        P("groups"),
        P("groups"),
        P("groups", None),
        P(None, "groups", "tensor"),
        P("tensor"),
        P("tensor"),
        P("tensor", "replica"),
        P("tensor", None, "replica"),
        P(None, "replica"),
        P("replica", "tensor"),
        P("tensor", None, "replica"),
        P("replica", "tensor"),
    )
    return jax.shard_map(
        per_device,
        mesh=mesh,
        in_specs=placed,
        out_specs=(P(None, "groups", "tensor"), P(None, ("groups", "tensor"), "replica")),
        check_vma=False,
    )
```

profile of v0, /device:TPU:0, one launch (start us, length us, event | category | flops | bytes accessed | tf_op | source)
XLA Modules:
  0.0 354.1 jit_solution(11194829674066063407)
XLA Ops:
  7.2 5.8 %fusion.34 = f32[32,1024]{1,0:T(8,128)} fusion(bf16[4096,1024]{1,0:T(8,128)(2,1)} %param.20, f32[4096]{0:T(1024)} %param.18, bf16[2,32,4096]{2,1,0:T(8,128)(2,1)} %param.17), kind=kOutput, calls=%fused_computation.62 | convolution fusion | flops 268828672 | bytes 8798208 | tf_op jit(solution)/shard_map/dot_general | solution.py:130
  13.1 3.2 fusion.39
  16.2 11.8 %copy.128 = bf16[512,8,2,1024]{3,1,2,0:T(8,128)(2,1)S(1)} copy(bf16[512,8,2,1024]{3,2,1,0:T(2,128)(2,1)} %bitcast.253) | data formatting | bytes 33554432
  28.0 4.5 %fusion.32 = f32[32,2048]{1,0:T(8,128)} fusion(bf16[4096,2048]{1,0:T(8,128)(2,1)S(1)} %bitcast.245, f32[4096]{0:T(1024)S(1)} %copy-done.5, bf16[2,32,4096]{2,1,0:T(8,128)(2,1)S(1)} %copy-done.2), kind=kOutput, calls=%fused_computation.61 | convolution fusion | flops 537264128 | bytes 17317888 | tf_op jit(solution)/shard_map/dot_general | solution.py:131
  32.6 1.3 copy-done
  33.8 3.7 %fusion.37 = f32[32,2048]{1,0:T(8,128)} fusion(bf16[4096,2048]{1,0:T(8,128)(2,1)S(1)} %bitcast.246, f32[4096]{0:T(1024)S(1)} %copy-done.5, bf16[2,32,4096]{2,1,0:T(8,128)(2,1)S(1)} %copy-done.2), kind=kOutput, calls=%fused_computation.64 | convolution fusion | flops 537264128 | bytes 17317888 | tf_op jit(solution)/shard_map/dot_general | solution.py:131
  38.3 0.9 scatter_custom_fusion.1
  39.2 34.9 %all-gather.6 = bf16[8,12,4096]{2,1,0:T(8,128)(2,1)S(1)} all-gather(bf16[1,12,4096]{2,1,0:T(8,128)(2,1)S(1)} %bitcast.273), channel_id=1, replica_groups=mesh['groups'=2,'replica'=8,'tensor'=2] {'replica'}, dimensions={0}, use_global_device_ids=true | all-gather | bytes 884736 | tf_op jit(solution)/shard_map/all_gather | solution.py:76
  74.2 8.5 %fusion.7 = f32[96,2048]{1,0:T(8,128)S(1)} fusion(bf16[4096,2048]{1,0:T(8,128)(2,1)} %bitcast.247, f32[96,4096]{1,0:T(8,128)S(1)} %reshape.388, f32[4096]{0:T(1024)S(1)} %copy-done.5), kind=kOutput, calls=%fused_computation.21 | convolution fusion | flops 1611399168 | bytes 19152896 | tf_op jit(solution)/shard_map/dot_general | solution.py:79
  82.7 3.0 scatter_custom_fusion.3
  85.7 2.4 convert_element_type.167
  88.3 0.2 multiply_reduce_fusion
  88.7 1.2 scatter_custom_fusion.2
  89.9 0.6 dynamic-slice
  91.2 0.9 scatter_custom_fusion
  92.1 0.2 fusion.17
  92.3 2.5 all-reduce.4
  94.7 2.4 all-reduce
  97.4 1.2 fusion.56
  98.8 1.0 fusion.57
  100.4 1.2 select_convert_fusion
  101.5 1.2 fusion.1
  102.7 0.3 fusion
  103.9 0.2 convert_convert_fusion
  104.4 1.8 all-gather.9
  106.3 1.8 all-gather.10
  108.2 1.8 all-gather.8
  110.0 1.8 all-gather.7
  113.1 0.3 fusion.2
  113.4 2.0 all-gather.3
  115.7 0.3 convolution_add_fusion.1
  116.0 2.0 all-gather
  118.3 5.9 %fusion.86 = f32[32,4096]{1,0:T(8,128)} fusion(bf16[1024,4096]{1,0:T(8,128)(2,1)} %param.23, f32[4,8,8,128]{3,2,1,0:T(8,128)S(1)} %bitcast.263, f32[4,8,8,128]{3,2,1,0:T(8,128)S(1)} %bitcast.259, f32[4,8,8,128]{3,2,1,0:T(8,128)S(1)} %bitcast.261, f32[64,1024]{1,0:T(8,128)S(1)} %all-gather.3), kind=kOutput, calls=%fused_computation.130 | convolution fusion | flops 268599296 | bytes 9568256 | tf_op jit(solution)/shard_map/dot_general | solution.py:179
  124.5 2.3 fusion.84
  126.9 0.3 all-reduce.16.cloned.1.call-start
  127.2 24.7 %copy.137 = bf16[512,8,2,1536]{3,1,2,0:T(8,128)(2,1)} copy(bf16[512,8,2,1536]{3,2,1,0:T(2,128)(2,1)} %bitcast.252) | data formatting | bytes 50331648
  151.8 54.4 %all-reduce.14.cloned.1.call-done = (f32[32,4096]{1,0:T(8,128)}, f32[32,4096]{1,0:T(8,128)}) async-done(((f32[32,4096]{1,0:T(8,128)}, f32[32,4096]{1,0:T(8,128)}), (f32[32,4096]{1,0:T(8,128)}, f32[32,4096]{1,0:T(8,128)})) %all-reduce.14.cloned.1.call-update) | async-done | bytes 1048592 | tf_op jit(solution)/shard_map/psum | solution.py:180
  206.3 13.6 %fusion.29 = f32[32,3072]{1,0:T(8,128)} fusion(bf16[4096,3072]{1,0:T(8,128)(2,1)} %bitcast.248, f32[4096]{0:T(1024)S(1)} %copy-done.7, f32[32,4096]{1,0:T(8,128)} %get-tuple-element.50, bf16[2,32,4096]{2,1,0:T(8,128)(2,1)S(1)} %copy-done.2), kind=kOutput, calls=%fused_computation.58 | convolution fusion | flops 805830656 | bytes 26361856 | tf_op jit(solution)/shard_map/dot_general | solution.py:182
  219.8 11.2 %fusion.27 = f32[32,3072]{1,0:T(8,128)} fusion(bf16[4096,3072]{1,0:T(8,128)(2,1)} %bitcast.249, f32[4096]{0:T(1024)S(1)} %copy-done.7, f32[32,4096]{1,0:T(8,128)S(1)} %copy-done.4, bf16[2,32,4096]{2,1,0:T(8,128)(2,1)S(1)} %copy-done.2), kind=kOutput, calls=%fused_computation.56 | convolution fusion | flops 805830656 | bytes 26361856 | tf_op jit(solution)/shard_map/dot_general | solution.py:182
  231.1 0.3 multiply_reduce_fusion.2
  231.4 2.5 all-reduce.3
  233.9 16.0 %all-reduce.16.cloned.1.call-done = (f32[32,3072]{1,0:T(8,128)}, f32[32,3072]{1,0:T(8,128)}) async-done(((f32[32,3072]{1,0:T(8,128)}, f32[32,3072]{1,0:T(8,128)}), (f32[32,3072]{1,0:T(8,128)}, f32[32,3072]{1,0:T(8,128)})) %all-reduce.16.cloned.1.call-update) | async-done | bytes 786448 | tf_op jit(solution)/shard_map/psum | solution.py:186
  249.9 8.0 %fusion.78 = f32[32,4096]{1,0:T(8,128)} fusion(bf16[1536,4096]{1,0:T(8,128)(2,1)} %param.25, f32[32,3072]{1,0:T(8,128)} %get-tuple-element.64, f32[32]{0:T(128)S(1)} %add_rsqrt_fusion), kind=kOutput, calls=%fused_computation.124 | convolution fusion | flops 403046400 | bytes 13500544 | tf_op jit(solution)/shard_map/dot_general | solution.py:191
  257.8 7.7 %fusion.76 = f32[32,4096]{1,0:T(8,128)} fusion(bf16[1536,4096]{1,0:T(8,128)(2,1)} %param.25, f32[32,3072]{1,0:T(8,128)S(1)} %copy-done.9, f32[32]{0:T(128)S(1)} %add_rsqrt_fusion.2), kind=kOutput, calls=%fused_computation.123 | convolution fusion | flops 403046400 | bytes 13500544 | tf_op jit(solution)/shard_map/dot_general | solution.py:191
  265.6 0.8 copy.172
  266.4 79.0 %all-reduce.12.cloned.1.call-done = (f32[32,4096]{1,0:T(8,128)}, f32[32,4096]{1,0:T(8,128)}) async-done(((f32[32,4096]{1,0:T(8,128)}, f32[32,4096]{1,0:T(8,128)}), (f32[32,4096]{1,0:T(8,128)}, f32[32,4096]{1,0:T(8,128)})) %all-reduce.12.cloned.1.call-update) | async-done | bytes 1048592 | tf_op jit(solution)/shard_map/psum | solution.py:192
  345.4 1.3 fusion.28
  346.7 0.8 pad_maximum_fusion
  (124 shorter events, 5.6 us)
Async XLA Ops:
  7.2 5.9 %copy-start.5 = (f32[4096]{0:T(1024)S(1)}, f32[4096]{0:T(1024)}, u32[]{:S(2)}) copy-start(f32[4096]{0:T(1024)} %param.18) | copy-start | bytes 49156
  7.2 90.2 %all-reduce.18.cloned.1.call-start = ((), (), s32[]{:S(2)}) async-start(), calls=%async_computation.5 | async-start | bytes 1572864 | tf_op jit(solution)/shard_map/psum | solution.py:133
  7.2 5.9 %copy-start.1 = (bf16[4096,1024]{1,0:T(8,128)(2,1)S(1)}, bf16[4096,1024]{1,0:T(8,128)(2,1)}, u32[]{:S(2)}) copy-start(bf16[4096,1024]{1,0:T(8,128)(2,1)} %param.20) | copy-start | bytes 25165828
  16.2 11.8 %copy-start.2 = (bf16[2,32,4096]{2,1,0:T(8,128)(2,1)S(1)}, bf16[2,32,4096]{2,1,0:T(8,128)(2,1)}, u32[]{:S(2)}) copy-start(bf16[2,32,4096]{2,1,0:T(8,128)(2,1)} %param.17) | copy-start | bytes 1572868
  28.0 5.8 %copy-start = (bf16[512,8,2,1024]{3,1,2,0:T(8,128)(2,1)}, bf16[512,8,2,1024]{3,1,2,0:T(8,128)(2,1)S(1)}, u32[]{:S(2)}) copy-start(bf16[512,8,2,1024]{3,1,2,0:T(8,128)(2,1)S(1)} %copy.128) | copy-start | bytes 50331652
  33.8 3.8 %copy-start.12 = (s32[32]{0:T(128)S(1)}, s32[32]{0:T(128)}, u32[]{:S(2)}) copy-start(s32[32]{0:T(128)} %param.14) | copy-start | bytes 388
  33.8 3.8 %copy-start.14 = (s32[32]{0:T(128)S(1)}, s32[32]{0:T(128)}, u32[]{:S(2)}) copy-start(s32[32]{0:T(128)} %param.15) | copy-start | bytes 388
  33.8 4.0 %copy-start.13 = (s32[32,3]{0,1:T(4,128)S(1)}, s32[32,3]{0,1:T(4,128)}, u32[]{:S(2)}) copy-start(s32[32,3]{0,1:T(4,128)} %param.16) | copy-start | bytes 1156
  33.8 5.3 %copy-start.10 = (bf16[12,4096]{1,0:T(8,128)(2,1)S(1)}, bf16[12,4096]{1,0:T(8,128)(2,1)}, u32[]{:S(2)}) copy-start(bf16[12,4096]{1,0:T(8,128)(2,1)} %param.13) | copy-start | bytes 294916
  37.6 62.8 %reduce-scatter.2.cloned.1.call-start = ((), (), s32[]{:S(2)}) async-start(), calls=%async_computation.1 | async-start | bytes 1179648 | tf_op jit(solution)/shard_map/reduce_scatter | solution.py:84
  74.2 14.1 %copy-start.11 = (f32[3,1024]{1,0:T(4,128)S(1)}, f32[3,1024]{1,0:T(4,128)}, u32[]{:S(2)}) copy-start(f32[3,1024]{1,0:T(4,128)} %param.22) | copy-start | bytes 36868
  74.2 15.7 %copy-start.15 = (u32[32]{0:T(128)S(1)}, u32[32]{0:T(128)}, u32[]{:S(2)}) copy-start(u32[32]{0:T(128)} %constant.88) | copy-start | bytes 388
  88.1 118.1 %all-reduce.14.cloned.1.call-start = ((), (), s32[]{:S(2)}) async-start(), calls=%async_computation.3 | async-start | bytes 2097152 | tf_op jit(solution)/shard_map/psum | solution.py:180
  97.4 15.7 %copy-start.6 = (f32[32,2048]{1,0:T(8,128)S(1)}, f32[32,2048]{1,0:T(8,128)}, u32[]{:S(2)}) copy-start(f32[32,2048]{1,0:T(8,128)} %get-tuple-element.69) | copy-start | bytes 786436
  97.4 15.7 %copy-start.8 = (f32[32,2048]{1,0:T(8,128)S(1)}, f32[32,2048]{1,0:T(8,128)}, u32[]{:S(2)}) copy-start(f32[32,2048]{1,0:T(8,128)} %get-tuple-element.68) | copy-start | bytes 786436
  118.2 6.3 %slice-start = ((s8[8388608]{0:T(1024)(128)(4,1)}), s8[4194304]{0:T(1024)(128)(4,1)S(1)}, s32[]{:S(2)}) async-start(s8[8388608]{0:T(1024)(128)(4,1)} %bitcast.250), calls=%async_computation.6 | async-start | bytes 8388608
  118.3 6.2 %slice-start.1 = ((s8[8388608]{0:T(1024)(128)(4,1)}), s8[4194304]{0:T(1024)(128)(4,1)S(1)}, s32[]{:S(2)}) async-start(s8[8388608]{0:T(1024)(128)(4,1)} %bitcast.250), calls=%async_computation.7 | async-start | bytes 8388608
  126.9 123.0 %all-reduce.16.cloned.1.call-start = ((), (), s32[]{:S(2)}) async-start(), calls=%async_computation.4 | async-start | bytes 1572864 | tf_op jit(solution)/shard_map/psum | solution.py:186
  127.1 79.1 %copy-start.7 = (f32[4096]{0:T(1024)S(1)}, f32[4096]{0:T(1024)}, u32[]{:S(2)}) copy-start(f32[4096]{0:T(1024)} %param.19) | copy-start | bytes 49156
  206.3 13.6 %copy-start.4 = (f32[32,4096]{1,0:T(8,128)S(1)}, f32[32,4096]{1,0:T(8,128)}, u32[]{:S(2)}) copy-start(f32[32,4096]{1,0:T(8,128)} %get-tuple-element.51) | copy-start | bytes 1572868
  219.8 11.3 %copy-start.3 = (f32[32,4096]{1,0:T(8,128)S(1)}, f32[32,4096]{1,0:T(8,128)}, u32[]{:S(2)}) copy-start(f32[32,4096]{1,0:T(8,128)} %get-tuple-element.50) | copy-start | bytes 1572868
  231.1 114.3 %all-reduce.12.cloned.1.call-start = ((), (), s32[]{:S(2)}) async-start(), calls=%async_computation.2 | async-start | bytes 2097152 | tf_op jit(solution)/shard_map/psum | solution.py:192
  249.9 8.0 %copy-start.9 = (f32[32,3072]{1,0:T(8,128)S(1)}, f32[32,3072]{1,0:T(8,128)}, u32[]{:S(2)}) copy-start(f32[32,3072]{1,0:T(8,128)} %get-tuple-element.65) | copy-start | bytes 1179652
Sparse Core Ops, SparseCore 0:
  37.7 21.8 all-reduce.17
  88.3 9.0 reduce-scatter.1
  127.0 79.2 all-reduce.13
  231.2 18.6 all-reduce.15
  265.7 79.6 all-reduce.11
where the time goes:
time: 355 us; the launch traced here: 354 us
  waiting for transfers between devices  150 us (42%)
  matrix products  77.1 us (22%)
  blocking collectives  53.4 us (15%)
  local copies, waits for them, and re-layouts  44.5 us (13%)
  between operations  15 us (4%)
  other arithmetic  14.1 us (4%)
    psum x1, waiting for transfers between devices, per_device(): result = middle + lax.psum(down_part, 'replica')  79 us
    psum x1, waiting for transfers between devices, per_device(): middle = x_wide + lax.psum(attn_part, 'replica')  54.4 us
    unnamed x48, local copies, waits for them, and re-layouts  38.8 us
    all_gather x1, blocking collectives, per_device(): block_rows = lax.all_gather(hidden, 'replica', axis=0, tiled=True)  34.9 us
    dot_general x2, matrix products, per_device(): jnp.dot(scaled_mid, w_gateup.reshape(half_width, 2 * units), preferred_el...  24.8 us
    psum x1, waiting for transfers between devices, per_device(): gate_up, mid_squares = lax.psum((gate_up, mid_squares), 'tensor')  16 us
    dot_general x2, matrix products, per_device(): down_part = jnp.dot(hidden_mid, w_down, preferred_element_type=jnp.float32)  15.7 us
    all_gather x6, blocking collectives, merged(): gathered = jax.tree.map(lambda a: lax.all_gather(a, axis), part)  11.2 us
  transfers between devices with their start and end apart: 5, of which 3 were waited for; matrix products, arithmetic and copies ran while one was open for 13% of the time, Pallas kernels for 0%

commit v1 on v0

--- a/solution.py
+++ b/solution.py
@@ -121,42 +121,50 @@
             first[2] * spread_out(scale_one) + second[2] * spread_out(scale_two),
         )
 
-    new_keys = []
-    new_vals = []
-    decoded_rows = []
+    new_count = STEPS * rollouts
+    x_wide = x_new.reshape(new_count, half_width).astype(jnp.float32)
+    scaled = (x_wide * norm_attn).astype(jnp.bfloat16)
+    query_part = jnp.dot(scaled, w_query, preferred_element_type=jnp.float32)
+    keyval_part = jnp.dot(scaled, keyval_flat, preferred_element_type=jnp.float32)
+    squares = jnp.sum(x_wide * x_wide, axis=1, keepdims=True)
+    fused = jnp.concatenate(
+        [query_part, keyval_part, jnp.broadcast_to(squares, (new_count, 128))], axis=1
+    )
+    fused = lax.psum(fused, "tensor")
+    step_scale = lax.rsqrt(fused[:, 3 * columns : 3 * columns + 1] / D + EPSILON)
+    rows_new = (step_scale * fused[:, : 3 * columns] + qkv_bias.reshape(1, 3 * columns)).astype(
+        jnp.bfloat16
+    )
+    rows_new = rows_new.reshape(STEPS, rollouts, 3 * columns)
+    queries = rows_new[:, :, :columns]
+    new_keys = rows_new[:, :, columns : 2 * columns]
+    new_vals = rows_new[:, :, 2 * columns :]
+    pooled_query = jnp.stack(
+        [
+            jnp.dot(onehot_half, queries[s], preferred_element_type=jnp.float32)
+            for s in range(STEPS)
+        ]
+    )
+    cache_all = jnp.sum(
+        (pooled_query * cache_keys[None]).reshape(STEPS, half_rows, heads_here, piece_width),
+        axis=-1,
+    )
+    new_all = jnp.sum(
+        (
+            queries.astype(jnp.float32)[:, None] * new_keys.astype(jnp.float32)[None]
+        ).reshape(STEPS, STEPS, rollouts, heads_here, piece_width),
+        axis=-1,
+    )
+    for bit_index in range(bit_count):
+        swapped = partner((cache_all, new_all), "replica", bit_index)
+        cache_all = cache_all + swapped[0]
+        new_all = new_all + swapped[1]
+    parts = []
     for turn_index in range(STEPS):
-        x_wide = x_new[turn_index].astype(jnp.float32)
-        scaled = (x_wide * norm_attn).astype(jnp.bfloat16)
-        query_part = jnp.dot(scaled, w_query, preferred_element_type=jnp.float32)
-        keyval_part = jnp.dot(scaled, keyval_flat, preferred_element_type=jnp.float32)
-        squares = jnp.sum(x_wide * x_wide, axis=1)
-        query_part, keyval_part, squares = lax.psum((query_part, keyval_part, squares), "tensor")
-        step_scale = lax.rsqrt(squares / D + EPSILON)[:, None]
-        query = (step_scale * query_part + qkv_bias[0]).astype(jnp.bfloat16)
-        new_keys.append((step_scale * keyval_part[:, :columns] + qkv_bias[1]).astype(jnp.bfloat16))
-        new_vals.append((step_scale * keyval_part[:, columns:] + qkv_bias[2]).astype(jnp.bfloat16))
-        query_wide = query.astype(jnp.float32)
-        picked_query = jnp.dot(onehot_half, query, preferred_element_type=jnp.float32)
-        cache_scores = jnp.sum(
-            (picked_query * cache_keys).reshape(half_rows, heads_here, piece_width), axis=-1
-        )
-        new_scores = jnp.stack(
-            [
-                jnp.sum(
-                    (query_wide * key_row.astype(jnp.float32)).reshape(
-                        rollouts, heads_here, piece_width
-                    ),
-                    axis=-1,
-                )
-                for key_row in new_keys
-            ]
-        )
-        for bit_index in range(bit_count):
-            swapped = partner((cache_scores, new_scores), "replica", bit_index)
-            cache_scores = cache_scores + swapped[0]
-            new_scores = new_scores + swapped[1]
-        cache_scores = jnp.where(filled, cache_scores * inverse, NEGATIVE)
-        new_scores = jnp.where(keep_new, new_scores * inverse, NEGATIVE)
+        cache_scores = jnp.where(filled, cache_all[turn_index] * inverse, NEGATIVE)
+        new_scores = jnp.where(
+            keep_new, new_all[turn_index, : turn_index + 1] * inverse, NEGATIVE
+        )
         segment_top = jnp.max(
             jnp.where(onehot[:, :, None], cache_scores[:, None, :], NEGATIVE), axis=0
         )
@@ -169,29 +177,39 @@
         )
         cache_rounded = spread_out(cache_weights.astype(jnp.bfloat16).astype(jnp.float32))
         accum = jnp.dot(onehot_wide.T, cache_rounded * cache_vals, precision=lax.Precision.HIGHEST)
-        for item_index in range(len(new_vals)):
+        for item_index in range(turn_index + 1):
             new_rounded = spread_out(
                 new_weights[item_index].astype(jnp.bfloat16).astype(jnp.float32)
             )
             accum = accum + new_rounded * new_vals[item_index].astype(jnp.float32)
-        peak_all, total_all, accum_all = merged((peak_val, totals, accum), "tensor", combine)
-        attended = (accum_all / spread_out(total_all)).astype(jnp.bfloat16)
-        attn_part = jnp.dot(attended, w_out, preferred_element_type=jnp.float32)
-        middle = x_wide + lax.psum(attn_part, "replica")
-        scaled_mid = (middle * norm_ffn).astype(jnp.bfloat16)
-        gate_up = jnp.dot(
-            scaled_mid, w_gateup.reshape(half_width, 2 * units), preferred_element_type=jnp.float32
-        )
-        mid_squares = jnp.sum(middle * middle, axis=1)
-        gate_up, mid_squares = lax.psum((gate_up, mid_squares), "tensor")
-        mid_scale = lax.rsqrt(mid_squares / D + EPSILON)[:, None]
-        gate_vals = mid_scale * gate_up[:, :units]
-        up_vals = mid_scale * gate_up[:, units:]
-        hidden_mid = (jax.nn.silu(gate_vals) * up_vals).astype(jnp.bfloat16)
-        down_part = jnp.dot(hidden_mid, w_down, preferred_element_type=jnp.float32)
-        result = middle + lax.psum(down_part, "replica")
-        decoded_rows.append(result.astype(jnp.bfloat16))
-    return (jnp.stack(decoded_rows), kv_out)
+        parts.append(jnp.concatenate([accum, totals, peak_val], axis=1))
+    mine = jnp.stack(parts).reshape(new_count, columns + 2 * heads_here)
+    both = lax.all_gather(mine, "tensor")
+
+    def split(block):
+        return block[:, columns + heads_here :], block[:, columns : columns + heads_here], block[:, :columns]
+
+    _, total_all, accum_all = combine(split(both[0]), split(both[1]))
+    attended = (accum_all / spread_out(total_all)).astype(jnp.bfloat16)
+    attn_part = jnp.dot(attended, w_out, preferred_element_type=jnp.float32)
+    middle = x_wide + lax.psum(attn_part, "replica")
+    scaled_mid = (middle * norm_ffn).astype(jnp.bfloat16)
+    gate_up = jnp.dot(
+        scaled_mid, w_gateup.reshape(half_width, 2 * units), preferred_element_type=jnp.float32
+    )
+    mid_squares = jnp.sum(middle * middle, axis=1, keepdims=True)
+    fused_mid = lax.psum(
+        jnp.concatenate([gate_up, jnp.broadcast_to(mid_squares, (new_count, 128))], axis=1),
+        "tensor",
+    )
+    mid_scale = lax.rsqrt(fused_mid[:, 2 * units : 2 * units + 1] / D + EPSILON)
+    gate_vals = mid_scale * fused_mid[:, :units]
+    up_vals = mid_scale * fused_mid[:, units : 2 * units]
+    hidden_mid = (jax.nn.silu(gate_vals) * up_vals).astype(jnp.bfloat16)
+    down_part = jnp.dot(hidden_mid, w_down, preferred_element_type=jnp.float32)
+    result = middle + lax.psum(down_part, "replica")
+    decoded = result.astype(jnp.bfloat16).reshape(STEPS, rollouts, half_width)
+    return (decoded, kv_out)
 
 
 def solution(mesh):

time: 355 us -> 323 us (0.910)
  matrix products: 77.1 us -> 49.7 us
  blocking collectives: 53.4 us -> 39.4 us
  other arithmetic: 14.1 us -> 18.6 us
    dot_general x2 -> x1, matrix products: 24.8 us -> 10.4 us  [per_device(): jnp.dot(scaled_mid, w_gateup.reshape(half_width, 2 * units), preferred_el...]
    all_gather x6 -> x1, blocking collectives: 11.2 us -> 2.23 us  [per_device(): both = lax.all_gather(mine, 'tensor')]
    dot_general x2 -> x1, matrix products: 15.7 us -> 8.32 us  [per_device(): down_part = jnp.dot(hidden_mid, w_down, preferred_element_type=jnp.float32)]
    convert_element_type x0 -> x4, other arithmetic: none -> 5.83 us  [the longest x2 2.38 us: per_device(): scaled = (x_wide * norm_attn).astype(jnp.bfloat16)]
    psum x2 -> x0, blocking collectives: 4.93 us -> none  [the longest x1 2.46 us: per_device(): lax.psum((query_part, keyval_part, squares), 'tensor')]
    unnamed x48 -> x29, local copies, waits for them, and re-layouts: 38.8 us -> 43.4 us
    dot_general x2 -> x1, matrix products: 8.99 us -> 4.99 us  [per_device(): query_part = jnp.dot(scaled, w_query, preferred_element_type=jnp.float32)]
    dot_general x2 -> x1, matrix products: 8.22 us -> 5.99 us  [per_device(): attn_part = jnp.dot(attended, w_out, preferred_element_type=jnp.float32)]
  transfers between devices with their start and end apart: 5 -> 5, of which waited for: 3 -> 3; matrix products, arithmetic and copies ran while one was open for 13% -> 15% of each run, Pallas kernels for 0% -> 0%
where the time goes in v1:
time: 323 us; the launch traced here: 322 us
  waiting for transfers between devices  152 us (47%)
  matrix products  49.7 us (15%)
  local copies, waits for them, and re-layouts  47.9 us (15%)
  blocking collectives  39.4 us (12%)
  other arithmetic  18.6 us (6%)
  between operations  15 us (5%)
    psum x1, waiting for transfers between devices, per_device(): result = middle + lax.psum(down_part, 'replica')  78.2 us
    psum x1, waiting for transfers between devices, per_device(): middle = x_wide + lax.psum(attn_part, 'replica')  54.3 us
    unnamed x29, local copies, waits for them, and re-layouts  43.4 us
    all_gather x1, blocking collectives, per_device(): block_rows = lax.all_gather(hidden, 'replica', axis=0, tiled=True)  34.7 us
    psum x1, waiting for transfers between devices, per_device(): lax.psum(jnp.concatenate([gate_up, jnp.broadcast_to(mid_squares, (new_cou...  19 us
    dot_general x1, matrix products, per_device(): jnp.dot(scaled_mid, w_gateup.reshape(half_width, 2 * units), preferred_el...  10.4 us
    dot_general x1, matrix products, per_device(): jnp.dot(make_scaled, keyval_flat, preferred_element_type=jnp.float32)  9.44 us
    dot_general x1, matrix products, per_device(): jnp.dot(scaled, keyval_flat, preferred_element_type=jnp.float32)  8.78 us
  transfers between devices with their start and end apart: 5, of which 3 were waited for; matrix products, arithmetic and copies ran while one was open for 15% of the time, Pallas kernels for 0%

profile of v1, /device:TPU:0, one launch (start us, length us, event | category | flops | bytes accessed | tf_op | source)
XLA Modules:
  0.0 322.5 jit_solution(14096516408157296283)
XLA Ops:
  7.2 1.2 fusion.3
  8.5 1.1 fusion.5
  9.6 17.1 %copy.66 = bf16[512,8,2,1024]{3,1,2,0:T(8,128)(2,1)} copy(bf16[512,8,2,1024]{3,2,1,0:T(2,128)(2,1)} %bitcast.184) | data formatting | bytes 33554432
  26.8 8.8 %fusion.88 = f32[64,2048]{1,0:T(8,128)S(1)} fusion(bf16[64,4096]{1,0:T(8,128)(2,1)S(1)} %bitcast.185, bf16[4096,2048]{1,0:T(8,128)(2,1)} %bitcast.180), kind=kOutput, calls=%fused_computation.162 | convolution fusion | flops 1073741824 | bytes 17825792 | tf_op jit(solution)/shard_map/dot_general | solution.py:128
  35.6 5.0 %fusion.87 = f32[64,1024]{1,0:T(8,128)S(1)} fusion(bf16[64,4096]{1,0:T(8,128)(2,1)S(1)} %fusion.5, bf16[4096,1024]{1,0:T(8,128)(2,1)} %param.20), kind=kOutput, calls=%fused_computation.161 | convolution fusion | flops 536870912 | bytes 9175040 | tf_op jit(solution)/shard_map/dot_general | solution.py:127
  40.7 1.0 pad_maximum_fusion
  41.8 0.2 select_reduce_fusion.2
  42.4 0.9 scatter_custom_fusion.1
  43.3 34.7 %all-gather = bf16[8,12,4096]{2,1,0:T(8,128)(2,1)S(1)} all-gather(bf16[1,12,4096]{2,1,0:T(8,128)(2,1)S(1)} %bitcast.207), channel_id=1, replica_groups=mesh['groups'=2,'replica'=8,'tensor'=2] {'replica'}, dimensions={0}, use_global_device_ids=true | all-gather | bytes 884736 | tf_op jit(solution)/shard_map/all_gather | solution.py:76
  78.0 0.2 reshape.380
  78.2 9.4 %fusion.6 = f32[96,2048]{1,0:T(8,128)} fusion(bf16[4096,2048]{1,0:T(8,128)(2,1)} %bitcast.181, f32[96,4096]{1,0:T(8,128)S(1)} %reshape.380, f32[4096]{0:T(1024)S(1)} %copy-done.2), kind=kOutput, calls=%fused_computation.29 | convolution fusion | flops 1611399168 | bytes 19152896 | tf_op jit(solution)/shard_map/dot_general | solution.py:79
  87.6 2.7 scatter_custom_fusion.3
  90.3 1.0 convert_element_type.120
  91.5 0.2 multiply_reduce_fusion
  91.9 1.2 scatter_custom_fusion.2
  93.1 2.5 all-reduce
  95.6 1.1 scatter_custom_fusion
  96.8 0.6 dynamic-slice
  98.1 0.9 fusion.44
  99.0 1.3 fusion.8
  100.4 0.2 multiply_reduce_fusion.2
  100.7 0.2 convolution_bitcast_fusion.1
  100.9 0.2 convolution_bitcast_fusion
  101.2 1.2 select_convert_fusion
  102.4 0.3 fusion.9
  102.8 0.1 select_reduce_fusion.1
  103.0 0.2 convert_convert_fusion.1
  103.2 0.2 convert_convert_fusion.2
  103.4 0.1 convolution_add_fusion.3
  103.8 0.2 broadcast_in_dim.197
  104.0 0.3 convolution_add_fusion.1
  104.4 0.1 convolution_add_fusion.2
  104.8 0.2 broadcast_in_dim.202
  104.9 0.3 fusion
  105.3 2.2 all_gather.7
  108.1 6.0 %fusion.29 = f32[64,4096]{1,0:T(8,128)} fusion(bf16[1024,4096]{1,0:T(8,128)(2,1)} %param.23, f32[8,8,8,128]{3,2,1,0:T(8,128)S(1)} %bitcast.192, f32[8,8,8,128]{3,2,1,0:T(8,128)S(1)} %bitcast.191, f32[8,8,8,128]{3,2,1,0:T(8,128)S(1)} %bitcast.190, f32[64,1040]{1,0:T(8,128)S(1)} %get-tuple-element.20, f32[64,1040]{1,0:T(8,128)S(1)} %get-tuple-element.19), kind=kOutput, calls=%fused_computation.69 | convolution fusion | flops 537198592 | bytes 10747904 | tf_op jit(solution)/shard_map/dot_general | solution.py:194
  114.2 24.7 %copy.78 = bf16[512,8,2,1536]{3,1,2,0:T(8,128)(2,1)} copy(bf16[512,8,2,1536]{3,2,1,0:T(2,128)(2,1)} %bitcast.183) | data formatting | bytes 50331648
  138.9 54.3 %all-reduce.8.cloned.1.call-done = f32[64,4096]{1,0:T(8,128)} async-done(((f32[64,4096]{1,0:T(8,128)}), f32[64,4096]{1,0:T(8,128)}) %all-reduce.8.cloned.1.call-update) | async-done | bytes 1048592 | tf_op jit(solution)/shard_map/psum | solution.py:195
  193.2 1.5 bitcast_add_fusion
  194.7 10.4 %fusion.13 = f32[64,3072]{1,0:T(8,128)S(1)} fusion(bf16[4096,3072]{1,0:T(8,128)(2,1)} %bitcast.182, f32[64,4096]{1,0:T(8,128)S(1)} %get-tuple-element.17, f32[4096]{0:T(1024)S(1)} %copy-done.4), kind=kOutput, calls=%fused_computation.39 | convolution fusion | flops 1611137024 | bytes 27017216 | tf_op jit(solution)/shard_map/dot_general | solution.py:197
  205.2 1.0 pad_maximum_fusion.1
  206.2 19.0 %all-reduce.10.cloned.1.call-done = f32[64,3200]{1,0:T(8,128)} async-done(((f32[64,3200]{1,0:T(8,128)}), f32[64,3200]{1,0:T(8,128)}) %all-reduce.10.cloned.1.call-update) | async-done | bytes 819216 | tf_op jit(solution)/shard_map/psum | solution.py:201
  225.2 0.9 fusion.39
  226.1 8.3 %fusion.23 = f32[64,4096]{1,0:T(8,128)} fusion(bf16[1536,4096]{1,0:T(8,128)(2,1)} %param.25, f32[64,3200]{1,0:T(8,128)} %all-reduce.10.cloned.1.call-done, f32[64]{0:T(128)S(1)} %fusion.39), kind=kOutput, calls=%fused_computation.62 | convolution fusion | flops 806092800 | bytes 14418176 | tf_op jit(solution)/shard_map/dot_general | solution.py:209
  234.5 0.3 reshape.335
  234.8 0.8 copy.60
  235.6 78.2 %all-reduce.12.cloned.1.call-done = f32[64,4096]{1,0:T(8,128)} async-done(((f32[64,4096]{1,0:T(8,128)}), f32[64,4096]{1,0:T(8,128)}) %all-reduce.12.cloned.1.call-update) | async-done | bytes 1048592 | tf_op jit(solution)/shard_map/psum | solution.py:210
  313.8 2.1 add_convert_fusion
  (78 shorter events, 2.8 us)
Async XLA Ops:
  7.2 90.9 %all-reduce.6.cloned.1.call-start = ((), (), s32[]{:S(2)}) async-start(), calls=%async_computation.1 | async-start | bytes 1638400 | tf_op jit(solution)/shard_map/psum | solution.py:133
  35.6 6.2 %copy-start.6 = (s32[32]{0:T(128)S(1)}, s32[32]{0:T(128)}, u32[]{:S(2)}) copy-start(s32[32]{0:T(128)} %param.14) | copy-start | bytes 388
  35.6 6.2 %copy-start.8 = (s32[32]{0:T(128)S(1)}, s32[32]{0:T(128)}, u32[]{:S(2)}) copy-start(s32[32]{0:T(128)} %param.15) | copy-start | bytes 388
  35.6 6.4 %copy-start.7 = (s32[32,3]{0,1:T(4,128)S(1)}, s32[32,3]{0,1:T(4,128)}, u32[]{:S(2)}) copy-start(s32[32,3]{0,1:T(4,128)} %param.16) | copy-start | bytes 1156
  35.6 7.7 %copy-start.3 = (bf16[12,4096]{1,0:T(8,128)(2,1)S(1)}, bf16[12,4096]{1,0:T(8,128)(2,1)}, u32[]{:S(2)}) copy-start(bf16[12,4096]{1,0:T(8,128)(2,1)} %param.13) | copy-start | bytes 294916
  35.6 42.5 %copy-start.2 = (f32[4096]{0:T(1024)S(1)}, f32[4096]{0:T(1024)}, u32[]{:S(2)}) copy-start(f32[4096]{0:T(1024)} %param.18) | copy-start | bytes 49156
  41.7 59.5 %reduce-scatter.2.cloned.1.call-start = ((), (), s32[]{:S(2)}) async-start(), calls=%async_computation.2 | async-start | bytes 1179648 | tf_op jit(solution)/shard_map/reduce_scatter | solution.py:84
  78.1 13.6 %copy-start.5 = (f32[3,1024]{1,0:T(4,128)S(1)}, f32[3,1024]{1,0:T(4,128)}, u32[]{:S(2)}) copy-start(f32[3,1024]{1,0:T(4,128)} %param.22) | copy-start | bytes 36868
  78.2 18.6 %copy-start.9 = (u32[32]{0:T(128)S(1)}, u32[32]{0:T(128)}, u32[]{:S(2)}) copy-start(u32[32]{0:T(128)} %constant.11) | copy-start | bytes 388
  91.3 101.9 %all-reduce.8.cloned.1.call-start = ((), (), s32[]{:S(2)}) async-start(), calls=%async_computation.3 | async-start | bytes 2097152 | tf_op jit(solution)/shard_map/psum | solution.py:195
  114.1 111.1 %all-reduce.10.cloned.1.call-start = ((), (), s32[]{:S(2)}) async-start(), calls=%async_computation.4 | async-start | bytes 1638400 | tf_op jit(solution)/shard_map/psum | solution.py:201
  114.2 79.0 %copy-start = (bf16[2,32,4096]{2,1,0:T(8,128)(2,1)S(1)}, bf16[2,32,4096]{2,1,0:T(8,128)(2,1)}, u32[]{:S(2)}) copy-start(bf16[2,32,4096]{2,1,0:T(8,128)(2,1)} %param.17) | copy-start | bytes 1572868
  114.2 80.5 %copy-start.4 = (f32[4096]{0:T(1024)S(1)}, f32[4096]{0:T(1024)}, u32[]{:S(2)}) copy-start(f32[4096]{0:T(1024)} %param.19) | copy-start | bytes 49156
  206.2 107.6 %all-reduce.12.cloned.1.call-start = ((), (), s32[]{:S(2)}) async-start(), calls=%async_computation.5 | async-start | bytes 2097152 | tf_op jit(solution)/shard_map/psum | solution.py:210
  226.1 87.7 %copy-start.1 = (f32[64,4096]{1,0:T(8,128)S(1)}, f32[64,4096]{1,0:T(8,128)}, u32[]{:S(2)}) copy-start(f32[64,4096]{1,0:T(8,128)} %all-reduce.8.cloned.1.call-done) | copy-start | bytes 3145732
Sparse Core Ops, SparseCore 0:
  41.8 21.9 all-reduce.5
  91.5 9.0 reduce-scatter.1
  114.3 78.9 all-reduce.7
  206.3 18.8 all-reduce.9
  234.6 79.1 all-reduce.11

commit v2 on v1

--- a/solution.py
+++ b/solution.py
@@ -1,6 +1,8 @@
 import jax
 import jax.numpy as jnp
 from jax import lax
+from jax.experimental import pallas as pl
+from jax.experimental.pallas import tpu as pltpu
 from jax.sharding import PartitionSpec as P
 
 D = 8192
@@ -212,6 +214,458 @@
     return (decoded, kv_out)
 
 
+def fused_kernel(
+    hid_ref, len_ref, src_ref, page_ref, x_ref, gain_ref, gain2_ref, bias_ref,
+    wq_hbm, wkv_hbm, wo_hbm, wgu_hbm, wd_hbm,
+    dec_ref, pool_ref,
+    area_a, area_b, area_c, hbuf, dacc, drecv, hacc, hsend, hrecv, sq, sqrecv,
+    att, kvb, qb, nkv, psend, precv, zsend, zrecv, ag, guacc, gurecv, sq2, sq2recv, hm,
+    wsem, hg_send, hg_fwd, hg_recv, ten_send, ten_recv,
+    p_send, p_recv, z_send, z_recv, ag_send, ag_fwd, ag_recv,
+):
+    f32 = jnp.float32
+    bf16 = jnp.bfloat16
+    replicas = lax.axis_size("replica")
+    depth = replicas // 2
+    half = x_ref.shape[1]
+    chunk = half // replicas
+    cols = wq_hbm.shape[1]
+    units = wd_hbm.shape[0]
+    news = x_ref.shape[0]
+    rolls = len_ref.shape[1]
+    pad = hid_ref.shape[0]
+    cached = replicas * pad
+    me = lax.axis_index("replica")
+    core = lax.axis_index("tensor")
+    zed = me // 2
+    ex = me % 2
+    pair = {"replica": me + 1 - 2 * ex}
+    other = {"tensor": 1 - core}
+    mesh_id = pl.DeviceIdType.MESH
+
+    def column(i):
+        return 2 * ((zed + i) % depth) + ex
+
+    wkv2 = wkv_hbm.reshape(2 * half, cols)
+    wgu2 = wgu_hbm.reshape(2 * half, units)
+    quarter = half // 2
+    wq_copies = [
+        pltpu.make_async_copy(
+            wq_hbm.at[pl.ds(i * quarter, quarter)], area_b.at[pl.ds(i * quarter, quarter)], wsem.at[i]
+        )
+        for i in range(2)
+    ]
+    wkv_copies = [
+        pltpu.make_async_copy(
+            wkv2.at[pl.ds(i * quarter, quarter)], area_a.at[pl.ds(i * quarter, quarter)], wsem.at[2 + i]
+        )
+        for i in range(4)
+    ]
+    wgu_copy = pltpu.make_async_copy(wgu2, area_c, wsem.at[6])
+    for copy in wq_copies + wkv_copies:
+        copy.start()
+
+    barrier = pltpu.get_barrier_semaphore()
+    pl.semaphore_signal(barrier, inc=1, device_id=pair, device_id_type=mesh_id)
+    pl.semaphore_signal(barrier, inc=1, device_id=other, device_id_type=mesh_id)
+    for i in range(1, depth):
+        pl.semaphore_signal(
+            barrier, inc=1, device_id={"replica": column(i)}, device_id_type=mesh_id
+        )
+    hbuf[me] = hid_ref[...]
+    pl.semaphore_wait(barrier, depth + 1)
+
+    def remote(src, dst, send, recv, target):
+        return pltpu.make_async_remote_copy(
+            src_ref=src, dst_ref=dst, send_sem=send, recv_sem=recv,
+            device_id=target, device_id_type=mesh_id,
+        )
+
+    def gather_start(buf, sends, recvs):
+        for i in range(1, depth):
+            remote(buf.at[me], buf.at[me], sends.at[i], recvs.at[me], {"replica": column(i)}).start()
+        remote(buf.at[me], buf.at[me], sends.at[0], recvs.at[me], pair).start()
+
+    def gather_step(n, buf, sends, fwds, recvs):
+        turn = n % depth
+        side = (ex + n // depth) % 2
+        block = 2 * ((zed - turn + depth) % depth) + side
+        arrived = remote(buf.at[block], buf.at[block], sends.at[0], recvs.at[block], pair)
+
+        @pl.when(n > 0)
+        def _():
+            arrived.wait_recv()
+
+        @pl.when((n > 0) & (n < depth))
+        def _():
+            remote(buf.at[block], buf.at[block], fwds.at[turn], recvs.at[block], pair).start()
+
+        return block
+
+    def gather_finish(buf, sends, fwds, recvs):
+        for i in range(depth):
+            remote(buf.at[me], buf.at[me], sends.at[i], recvs.at[me], pair).wait_send()
+        for i in range(1, depth):
+            remote(buf.at[me], buf.at[me], fwds.at[i], recvs.at[me], pair).wait_send()
+
+    gather_start(hbuf, hg_send, hg_recv)
+    wgu_copy.start()
+
+    step = min(512, chunk)
+    sq[pl.ds(0, news)] = jnp.zeros((news, 128), f32)
+
+    @pl.loop(0, half // step)
+    def _(k):
+        at = pl.ds(pl.multiple_of(k * step, step), step)
+        wide = x_ref[:, at].astype(f32)
+        sq[pl.ds(0, news)] += jnp.broadcast_to(
+            jnp.sum(wide * wide, axis=1, keepdims=True), (news, 128)
+        )
+
+    def scaled_new(at):
+        return (x_ref[:, at].astype(f32) * gain_ref[:, at]).astype(bf16)
+
+    spread_row = 2 * lax.broadcasted_iota(jnp.int32, (256, 512), 0)
+    spread_col = lax.broadcasted_iota(jnp.int32, (256, 512), 1)
+    even = (spread_col == spread_row).astype(bf16)
+    odd = (spread_col == spread_row + 1).astype(bf16)
+
+    def interleaved(piece):
+        sides = []
+        for each in (even, odd):
+            outs = [
+                jnp.dot(piece[:, j : j + 256], each, preferred_element_type=f32).astype(bf16)
+                for j in range(0, piece.shape[1], 256)
+            ]
+            sides.append(jnp.concatenate(outs, axis=1))
+        return jnp.concatenate(sides, axis=0)
+
+    dacc[...] = jnp.zeros_like(dacc)
+    for i in range(2):
+        wq_copies[i].wait()
+
+        @pl.loop(i * quarter // step, (i + 1) * quarter // step)
+        def _(k):
+            at = pl.ds(pl.multiple_of(k * step, step), step)
+            dacc[pl.ds(0, news)] += jnp.dot(scaled_new(at), area_b[at], preferred_element_type=f32)
+
+    wo_copies = [
+        pltpu.make_async_copy(
+            wo_hbm.at[:, pl.ds(i * cols, cols)], area_b.at[pl.ds(i * cols, cols)], wsem.at[7 + i]
+        )
+        for i in range(depth)
+    ]
+    for copy in wo_copies:
+        copy.start()
+    for i in range(4):
+        wkv_copies[i].wait()
+
+        @pl.loop(i * quarter // (2 * step), (i + 1) * quarter // (2 * step))
+        def _(k):
+            at = pl.ds(pl.multiple_of(k * step, step), step)
+            at2 = pl.ds(pl.multiple_of(k * 2 * step, 2 * step), 2 * step)
+            dacc[pl.ds(news, 2 * news)] += jnp.dot(
+                interleaved(scaled_new(at)), area_a[at2], preferred_element_type=f32
+            )
+
+    swap_new = remote(dacc, drecv, ten_send.at[0], ten_recv.at[0], other)
+    swap_new.start()
+
+    @pl.loop(0, replicas)
+    def _(n):
+        block = gather_step(n, hbuf, hg_send, hg_fwd, hg_recv)
+        rows = hbuf[block].astype(f32)
+        sq[pl.ds(pl.multiple_of(news + block * pad, pad), pad)] = jnp.broadcast_to(
+            jnp.sum(rows * rows, axis=1, keepdims=True), (pad, 128)
+        )
+
+    swap_sq = remote(sq, sqrecv, ten_send.at[1], ten_recv.at[1], other)
+    swap_sq.start()
+    hacc[...] = jnp.zeros_like(hacc)
+
+    @pl.loop(0, half // step)
+    def _(k):
+        at = pl.ds(pl.multiple_of(k * step, step), step)
+        at2 = pl.ds(pl.multiple_of(k * 2 * step, 2 * step), 2 * step)
+        rows = hbuf[:, :, at].reshape(cached, step).astype(f32)
+        scaled = (rows * gain_ref[:, at]).astype(bf16)
+        hacc[...] += jnp.dot(interleaved(scaled), area_a[at2], preferred_element_type=f32)
+
+    hsend[...] = hacc[...].astype(bf16)
+    swap_kv = remote(hsend, hrecv, ten_send.at[2], ten_recv.at[2], other)
+    swap_kv.start()
+    wd_copies = [
+        pltpu.make_async_copy(
+            wd_hbm.at[:, pl.ds(i * cols, cols)], area_a.at[pl.ds(i * units, units)],
+            wsem.at[7 + depth + i],
+        )
+        for i in range(depth)
+    ]
+    for copy in wd_copies:
+        copy.start()
+
+    square = (rolls, rolls)
+    row_id = lax.broadcasted_iota(jnp.int32, square, 0)
+    col_id = lax.broadcasted_iota(jnp.int32, square, 1)
+    eye = row_id == col_id
+
+    def upright(row):
+        return jnp.sum(jnp.where(eye, row.astype(f32), 0.0), axis=1, keepdims=True)
+
+    lengths = upright(len_ref[...])
+    sources = upright(src_ref[...])
+    earlier = (sources == src_ref[...].astype(f32)) & (col_id < row_id)
+    offset = jnp.sum(jnp.where(earlier, len_ref[...].astype(f32), 0.0), axis=1, keepdims=True)
+    slot = lax.broadcasted_iota(jnp.int32, (rolls, cached), 1)
+    place = (slot % pad).astype(f32) - offset
+    match = ((slot // pad).astype(f32) == sources) & (place >= 0.0) & (place < lengths)
+    roll = lax.broadcasted_iota(jnp.int32, (rolls, cached), 0).astype(f32)
+    owner = jnp.max(jnp.where(match, roll, -1.0), axis=0, keepdims=True)
+    page = jnp.full((1, cached), -1.0, f32)
+    for p in range(page_ref.shape[0]):
+        picked = jnp.where(match & (place == p), upright(page_ref[pl.ds(p, 1)]), -1.0)
+        page = jnp.maximum(page, jnp.max(picked, axis=0, keepdims=True))
+
+    swap_new.wait()
+    swap_sq.wait()
+    totals = sq[...] + sqrecv[...]
+    scale = lax.rsqrt(totals / D + EPSILON)[:, :1]
+    new_scale = scale[:news]
+    qb[...] = (
+        new_scale * (dacc[pl.ds(0, news)] + drecv[pl.ds(0, news)]) + bias_ref[pl.ds(0, 1)]
+    ).astype(bf16)
+    for j in range(2):
+        at = pl.ds((1 + j) * news, news)
+        nkv[j] = (new_scale * (dacc[at] + drecv[at]) + bias_ref[pl.ds(1 + j, 1)]).astype(bf16)
+    swap_kv.wait()
+    for j in range(2):
+        at = pl.ds(j * cached, cached)
+        kvb[j] = (
+            scale[news:] * (hacc[at] + hrecv[at].astype(f32)) + bias_ref[pl.ds(1 + j, 1)]
+        ).astype(bf16)
+
+    half_pool = pool_ref.shape[1]
+    pick = (
+        lax.broadcasted_iota(jnp.int32, (half_pool, cached), 0) + core * half_pool
+    ).astype(f32) == page
+    pick = pick.astype(bf16)
+    for j in range(2):
+        pool_ref[j] = jnp.dot(pick, kvb[j], preferred_element_type=f32).astype(bf16)
+
+    token = lax.broadcasted_iota(jnp.int32, (news, cached), 0) % rolls
+    old_ok = token.astype(f32) == owner
+    t_row = lax.broadcasted_iota(jnp.int32, (news, news), 0)
+    t_col = lax.broadcasted_iota(jnp.int32, (news, news), 1)
+    new_ok = (t_row % rolls == t_col % rolls) & (t_col <= t_row)
+    inverse = 1.0 / jnp.sqrt(jnp.float32(HD))
+    across = (((1,), (1,)), ((), ()))
+    for h in range(cols // HD):
+        at = pl.ds(h * HD, HD)
+        q = qb[:, at]
+        old = lax.dot_general(q, kvb[0, :, at], across, preferred_element_type=f32)
+        new = lax.dot_general(q, nkv[0, :, at], across, preferred_element_type=f32)
+        old = jnp.where(old_ok, old * inverse, NEGATIVE)
+        new = jnp.where(new_ok, new * inverse, NEGATIVE)
+        peak = jnp.maximum(
+            jnp.max(old, axis=1, keepdims=True), jnp.max(new, axis=1, keepdims=True)
+        )
+        old = jnp.exp(old - peak)
+        new = jnp.exp(new - peak)
+        total = jnp.sum(old, axis=1, keepdims=True) + jnp.sum(new, axis=1, keepdims=True)
+        mixed = jnp.dot(old.astype(bf16), kvb[1, :, at], preferred_element_type=f32) + jnp.dot(
+            new.astype(bf16), nkv[1, :, at], preferred_element_type=f32
+        )
+        att[:, at] = (mixed / total).astype(bf16)
+
+    def reduce_chunks(which, lhs, area, depth_rows):
+        def partial(zc, side):
+            rows = pl.ds(pl.multiple_of(zc * depth_rows, depth_rows), depth_rows)
+            lanes = pl.ds(pl.multiple_of(side * chunk, chunk), chunk)
+            return jnp.dot(lhs[...], area[rows, lanes], preferred_element_type=f32)
+
+        def to_pair(i):
+            return remote(
+                psend.at[i], precv.at[which, i], p_send.at[which, i], p_recv.at[which, i], pair
+            )
+
+        def to_column(i):
+            return remote(
+                zsend.at[i], zrecv.at[which, i], z_send.at[which, i], z_recv.at[which, i],
+                {"replica": column(i)},
+            )
+
+        @pl.loop(1, depth + 1)
+        def _(n):
+            i = n % depth
+            psend[i] = partial((zed + i) % depth, 1 - ex).astype(bf16)
+            to_pair(i).start()
+
+        @pl.loop(1, depth)
+        def _(i):
+            mine = partial((zed + i) % depth, ex)
+            to_pair(i).wait_recv()
+            zsend[i] = (mine + precv[which, i].astype(f32)).astype(bf16)
+            to_column(i).start()
+
+        result = partial(zed, ex)
+        to_pair(0).wait_recv()
+        result = result + precv[which, 0].astype(f32)
+        for i in range(1, depth):
+            to_column(i).wait_recv()
+            result = result + zrecv[which, i].astype(f32)
+        for i in range(depth):
+            to_pair(i).wait_send()
+            if i:
+                to_column(i).wait_send()
+        return result
+
+    for copy in wo_copies:
+        copy.wait()
+    my_lanes = pl.ds(pl.multiple_of(me * chunk, chunk), chunk)
+    ag[0, me] = reduce_chunks(0, att, area_b, cols).astype(bf16)
+    first = (ag.at[0], ag_send.at[0], ag_fwd.at[0], ag_recv.at[0])
+    gather_start(first[0], first[1], first[3])
+    guacc[...] = jnp.zeros_like(guacc)
+    sq2[...] = jnp.zeros_like(sq2)
+    wgu_copy.wait()
+
+    @pl.loop(0, replicas)
+    def _(n):
+        block = gather_step(n, *first)
+        lanes = pl.ds(pl.multiple_of(block * chunk, chunk), chunk)
+        middle = x_ref[:, lanes].astype(f32) + ag[0, block].astype(f32)
+        sq2[...] += jnp.broadcast_to(jnp.sum(middle * middle, axis=1, keepdims=True), (news, 128))
+        scaled = (middle * gain2_ref[:, lanes]).astype(bf16)
+        rows = pl.ds(pl.multiple_of(block * 2 * chunk, 2 * chunk), 2 * chunk)
+        guacc[...] += jnp.dot(interleaved(scaled), area_c[rows], preferred_element_type=f32)
+
+    swap_gu = remote(guacc, gurecv, ten_send.at[3], ten_recv.at[3], other)
+    swap_sq2 = remote(sq2, sq2recv, ten_send.at[4], ten_recv.at[4], other)
+    swap_gu.start()
+    swap_sq2.start()
+    gather_finish(*first)
+    for copy in wd_copies:
+        copy.wait()
+    swap_sq2.wait()
+    mid_scale = lax.rsqrt((sq2[...] + sq2recv[...]) / D + EPSILON)[:, :1]
+    swap_gu.wait()
+    gate = mid_scale * (guacc[pl.ds(0, news)] + gurecv[pl.ds(0, news)])
+    up = mid_scale * (guacc[pl.ds(news, news)] + gurecv[pl.ds(news, news)])
+    hm[...] = (jax.nn.silu(gate) * up).astype(bf16)
+
+    down = reduce_chunks(1, hm, area_a, units)
+    middle = x_ref[:, my_lanes].astype(f32) + ag[0, me].astype(f32)
+    ag[1, me] = (middle + down).astype(bf16)
+    second = (ag.at[1], ag_send.at[1], ag_fwd.at[1], ag_recv.at[1])
+    gather_start(second[0], second[1], second[3])
+
+    @pl.loop(0, replicas)
+    def _(n):
+        block = gather_step(n, *second)
+        dec_ref[:, pl.ds(pl.multiple_of(block * chunk, chunk), chunk)] = ag[1, block]
+
+    gather_finish(*second)
+    gather_finish(hbuf, hg_send, hg_fwd, hg_recv)
+
+
+def fused_device(
+    hidden, rollout_lengths, source_replica, page_table, x_new, norm_attn, norm_ffn,
+    w_query, w_keyval, qkv_bias, w_out, w_gateup, w_down,
+):
+    replicas = lax.axis_size("replica")
+    depth = replicas // 2
+    slots, half = hidden.shape
+    pad = -(-slots // 16) * 16
+    cols = w_query.shape[1]
+    units = w_down.shape[0]
+    rolls, longest = page_table.shape
+    news = STEPS * rolls
+    cached = replicas * pad
+    chunk = half // replicas
+    f32, bf16 = jnp.float32, jnp.bfloat16
+    vm = pltpu.VMEM
+    dma = pltpu.SemaphoreType.DMA
+    in_vmem = pl.BlockSpec(memory_space=pltpu.VMEM)
+    in_hbm = pl.BlockSpec(memory_space=pl.ANY)
+    decoded, pool = pl.pallas_call(
+        fused_kernel,
+        out_shape=(
+            jax.ShapeDtypeStruct((news, half), bf16),
+            jax.ShapeDtypeStruct((2, rolls * longest, cols), bf16),
+        ),
+        in_specs=[in_vmem] * 8 + [in_hbm] * 5,
+        out_specs=(in_vmem, in_vmem),
+        scratch_shapes=[
+            vm((2 * half, cols), bf16),
+            vm((half, cols), bf16),
+            vm((2 * half, units), bf16),
+            vm((replicas, pad, half), bf16),
+            vm((3 * news, cols), f32),
+            vm((3 * news, cols), f32),
+            vm((2 * cached, cols), f32),
+            vm((2 * cached, cols), bf16),
+            vm((2 * cached, cols), bf16),
+            vm((news + cached, 128), f32),
+            vm((news + cached, 128), f32),
+            vm((news, cols), bf16),
+            vm((2, cached, cols), bf16),
+            vm((news, cols), bf16),
+            vm((2, news, cols), bf16),
+            vm((depth, news, chunk), bf16),
+            vm((2, depth, news, chunk), bf16),
+            vm((depth, news, chunk), bf16),
+            vm((2, depth, news, chunk), bf16),
+            vm((2, replicas, news, chunk), bf16),
+            vm((2 * news, units), f32),
+            vm((2 * news, units), f32),
+            vm((news, 128), f32),
+            vm((news, 128), f32),
+            vm((news, units), bf16),
+            dma((7 + 2 * depth,)),
+            dma((depth,)),
+            dma((depth,)),
+            dma((replicas,)),
+            dma((5,)),
+            dma((5,)),
+            dma((2, depth)),
+            dma((2, depth)),
+            dma((2, depth)),
+            dma((2, depth)),
+            dma((2, depth)),
+            dma((2, depth)),
+            dma((2, replicas)),
+        ],
+        compiler_params=pltpu.CompilerParams(
+            collective_id=0, has_side_effects=True, vmem_limit_bytes=VMEM_BYTES
+        ),
+        name="migrate_and_decode",
+    )(
+        jnp.pad(hidden, ((0, pad - slots), (0, 0))),
+        rollout_lengths.reshape(1, rolls),
+        source_replica.reshape(1, rolls),
+        page_table.T,
+        x_new.reshape(news, half),
+        norm_attn.reshape(1, half),
+        norm_ffn.reshape(1, half),
+        qkv_bias,
+        w_query,
+        w_keyval,
+        w_out,
+        w_gateup,
+        w_down,
+    )
+    return decoded.reshape(STEPS, rolls, half), pool
+
+
+VMEM_BYTES = 63 * 2**20
+
+
+def fits(mesh):
+    replicas = mesh.shape["replica"]
+    cols = D // replicas
+    return replicas % 2 == 0 and replicas <= 8 and cols % (2 * HD) == 0 and cols <= 1024
+
+
 def solution(mesh):
     placed = (
         P(("groups", "replica"), "tensor"),
@@ -229,7 +683,7 @@
         P("replica", "tensor"),
     )
     return jax.shard_map(
-        per_device,
+        fused_device if fits(mesh) else per_device,
         mesh=mesh,
         in_specs=placed,
         out_specs=(P(None, "groups", "tensor"), P(None, ("groups", "tensor"), "replica")),

time: 323 us -> 93.8 us (0.29)
  waiting for transfers between devices: 152 us -> 0 us
  Pallas kernels: 0 us -> 87.7 us
  matrix products: 49.7 us -> 0 us
  local copies, waits for them, and re-layouts: 47.9 us -> 5.21 us
  blocking collectives: 39.4 us -> 0 us
  other arithmetic: 18.6 us -> 0 us
  between operations: 15 us -> 0.64 us
    psum x4 -> x0, waiting for transfers between devices: 152 us -> none  [the longest x1 78.2 us: per_device(): result = middle + lax.psum(down_part, 'replica')]
    pallas_call x0 -> x1, Pallas kernels: none -> 87.7 us  [fused_device(): pl.pallas_call(fused_kernel, out_shape=(jax.ShapeDtypeStruct((news, half)...]
    dot_general x14 -> x0, matrix products: 49.7 us -> none  [the longest x1 10.4 us: per_device(): jnp.dot(scaled_mid, w_gateup.reshape(half_width, 2 * units), preferred_el...]
    unnamed x29 -> x2, local copies, waits for them, and re-layouts: 43.4 us -> 3.63 us
    all_gather x2 -> x0, blocking collectives: 36.9 us -> none  [the longest x1 34.7 us: per_device(): block_rows = lax.all_gather(hidden, 'replica', axis=0, tiled=True)]
    convert_element_type x9 -> x0, other arithmetic: 8.01 us -> none  [the longest x2 2.38 us: per_device(): scaled = (x_wide * norm_attn).astype(jnp.bfloat16)]
    scatter-add x2 -> x0, other arithmetic: 3.95 us -> none  [the longest x1 2.73 us: per_device(): part_pool = empty[0].at[lookup].add(partial_kv, mode='drop')]
  transfers between devices with their start and end apart: 5 -> 0, of which waited for: 3 -> 0; matrix products, arithmetic and copies ran while one was open for 15% -> 0% of each run, Pallas kernels for 0% -> 0%
where the time goes in v2:
time: 93.8 us; the launch traced here: 93.5 us
  Pallas kernels  87.7 us (93%)
  local copies, waits for them, and re-layouts  5.21 us (6%)
    pallas_call x1, Pallas kernels, fused_device(): pl.pallas_call(fused_kernel, out_shape=(jax.ShapeDtypeStruct((news, half)...  87.7 us
    unnamed x2, local copies, waits for them, and re-layouts  3.63 us

profile of v2, /device:TPU:0, one launch (start us, length us, event | category | flops | bytes accessed | tf_op | source)
XLA Modules:
  0.0 93.5 jit_solution(11345669775410906501)
XLA Ops:
  0.6 1.6 %pad.4.hid_ref = bf16[16,4096]{1,0:T(8,128)(2,1)} pad(bf16[12,4096]{1,0:T(8,128)(2,1)} %param.13, bf16[]{:T(256)} %constant.2.clone.1), padding=0_4x0_0 | pad | bytes 229378 | tf_op jit(solution)/shard_map/jit(_pad)/pad | solution.py:643
  2.2 87.7 %migrate_and_decode.1 = (bf16[64,4096]{1,0:T(8,128)(2,1)}, bf16[2,96,1024]{2,1,0:T(8,128)(2,1)}) custom-call(bf16[16,4096]{1,0:T(8,128)(2,1)} %pad.4.hid_ref, s32[1,32]{1,0:T(1,128)} %bitcast.12, s32[1,32]{1,0:T(1,128)} %bitcast.13, s32[3,32]{1,0:T(4,128)} %bitcast.11, bf16[64,4096]{1,0:T(8,128)(2,1)} %bitcast.7, f32[1,4096]{1,0:T(1,128)} %bitcast.9, ...), custom_call_target="tpu_custom_call" | custom-call | tf_op jit(solution)/shard_map/migrate_and_decode/pallas_call | solution.py:590
  89.9 1.9 %copy.17 = bf16[2,32,4096]{2,1,0:T(8,128)(2,1)} copy(bf16[2,32,4096]{2,1,0:T(8,128)(2,1)} %bitcast.8) | data formatting | bytes 1048576
  91.8 1.8 %copy.18 = bf16[2,96,1024]{2,1,0:T(8,128)(2,1)} copy(bf16[2,96,1024]{2,1,0:T(8,128)(2,1)} %get-tuple-element.9) | data formatting | bytes 786432
